TPU v7x, 32 devices: a whole 2x2x4 slice. The times are simulated.
32 devices in a mesh: dp: 8 (over z, x), bank: 4 (over y, core).
Axes of the slice: x: 2, y: 2, z: 4, core: 2. Of those that a mesh axis runs over, the one named last changes fastest.
Arguments:
- features: float32 [128, 128], P('dp'), may hold values from -6 to 6
- video_ids: int32 [8, 16], P('dp'), may hold values from 0 to 4, never falling along the last dimension, each value on 1 to 8 neighbouring positions
- bank: float32 [16384, 128], P(('dp', 'bank')), may hold values from -6 to 6
- loss_weight: float32 [128], P('dp'), may hold values from 0.5 to 2
Outputs:
- loss: float32 [128], P('dp')
- feature_grad: float32 [128, 128], P('dp')
Inputs may be any that keep to these rules, and one draw needn't show every extreme that they name: `video_ids`: each row of 16 frames holds 5 videos as runs of equal ids in ascending order, each video 1 to 8 frames and one exactly 8.
All inputs are finite; a program needn't handle non-finite values.
Results may differ from a plain program's by a relative error of at most 0.0003.
Values sent between devices are 32-bit elements; how exact they have to be, the bound alone decides.
A program may use at most 64 MiB of HBM per device.

v0:
```python
import math
import jax
import jax.numpy as jnp
from jax import lax
from jax.sharding import PartitionSpec as P

EPSILON = 1e-06
TAU_BACK = 0.1
HIGHEST = lax.Precision.HIGHEST


def unit_rows(values):
    return values / jnp.sqrt(jnp.sum(values * values, axis=1, keepdims=True) + EPSILON)


def cycle_loss(neighbour, normed, videos):
    frames = videos.shape[0]
    same_video = videos[:, None] == videos[None, :]
    row_index = lax.broadcasted_iota(jnp.int32, (frames, frames), 0)
    col_index = lax.broadcasted_iota(jnp.int32, (frames, frames), 1)
    earlier = same_video & (col_index < row_index)
    position = jnp.sum(jnp.where(earlier, 1.0, 0.0), axis=1).astype(neighbour.dtype)
    products = jnp.dot(neighbour, normed.T, precision=HIGHEST)
    distance = (
        jnp.sum(neighbour * neighbour, axis=1)[:, None]
        - 2.0 * products
        + jnp.sum(normed * normed, axis=1)[None, :]
    )
    back_weight = jnp.where(same_video, jnp.exp(-distance / TAU_BACK), 0.0)
    back_weight = back_weight / jnp.sum(back_weight, axis=1, keepdims=True)
    mean_pos = jnp.dot(back_weight, position, precision=HIGHEST)
    square_pos = jnp.dot(back_weight, position * position, precision=HIGHEST)
    spread = jnp.maximum(square_pos - mean_pos * mean_pos, 1.0)
    return (position - mean_pos) ** 2 / spread + 0.5 * jnp.log(spread)


def reduce_owner(partials):
    whole = lax.psum(partials, "bank")
    return lax.psum_scatter(whole, "dp", scatter_dimension=0, tiled=True)


def shards(features, video_ids, bank, loss_weight):
    per_owner, width = features.shape
    owners = lax.axis_size("dp")
    sharpness = 3.0 * math.sqrt(width)
    lengths = jnp.sqrt(jnp.sum(features * features, axis=1, keepdims=True) + EPSILON)
    normed = features / lengths
    keys = unit_rows(bank)
    gathered = lax.all_gather(normed, "dp", axis=0, tiled=True)
    group = 1
    while owners % (group * 2) == 0 and per_owner * group * 2 <= 512:
        group = group * 2
    step_rows = per_owner * group
    query_blocks = gathered.reshape(-1, step_rows, width)

    def forward_block(query_block):
        exp_scores = jnp.exp(sharpness * jnp.dot(query_block, keys.T, precision=HIGHEST))
        return (jnp.dot(exp_scores, keys, precision=HIGHEST), jnp.sum(exp_scores, axis=1))

    summed, partition = lax.map(forward_block, query_blocks)
    summed, partition = reduce_owner((summed.reshape(-1, width), partition.reshape(-1)))
    neighbour = summed / partition[:, None]
    loss, pullback = jax.vjp(
        lambda soft_rows, unit_part: cycle_loss(soft_rows, unit_part, video_ids[0]),
        neighbour,
        normed,
    )
    grad_soft, grad_local = pullback(loss_weight)
    gathered_grad = lax.all_gather(grad_soft, "dp", axis=0, tiled=True)
    grad_blocks = gathered_grad.reshape(-1, step_rows, width)

    def backward_block(paired):
        query_block, grad_block = paired
        exp_scores = jnp.exp(sharpness * jnp.dot(query_block, keys.T, precision=HIGHEST))
        projected = jnp.dot(grad_block, keys.T, precision=HIGHEST)
        return jnp.dot(exp_scores * projected, keys, precision=HIGHEST)

    moment = lax.map(backward_block, (query_blocks, grad_blocks)).reshape(-1, width)
    moment = reduce_owner((moment,))[0]
    along = jnp.sum(grad_soft * neighbour, axis=1, keepdims=True)
    grad_unit = grad_local + sharpness * (moment / partition[:, None] - along * neighbour)
    feature_grad = (
        grad_unit - normed * jnp.sum(normed * grad_unit, axis=1, keepdims=True)
    ) / lengths
    return (loss, feature_grad)


def solution(mesh):
    return jax.shard_map(
        shards,
        mesh=mesh,
        in_specs=(P("dp", None), P("dp", None), P(("dp", "bank"), None), P("dp")),
        out_specs=(P("dp"), P("dp", None)),
        check_vma=False,
    )
```

profile of v0, /device:TPU:0, one launch (start us, length us, event | category | flops | bytes accessed | tf_op | source)
XLA Modules:
  0.0 221.4 jit_solution(16359548754769475887)
XLA Ops:
  7.2 0.0 copy-start
  7.2 0.0 reduce-scatter.3.cloned.1.call-start
  7.2 0.8 multiply_reduce_fusion.6
  8.1 0.0 copy-start.1
  8.1 1.1 multiply_reduce_fusion
  9.2 0.0 copy-done.1
  9.2 0.2 multiply_reduce_fusion.4
  9.4 32.3 %all_gather.6 = f32[128,128]{1,0:T(8,128)S(1)} all-gather(f32[16,128]{1,0:T(8,128)S(1)} %get-tuple-element.42), channel_id=1, replica_groups=mesh['dp'=8,'bank'=4] {'dp'}, dimensions={0}, use_global_device_ids=true | all-gather | bytes 73728 | tf_op jit(solution)/shard_map/all_gather | solution.py:49
  41.7 0.0 copy-done
  41.7 0.6 fusion.28
  42.3 1.1 fusion.25
  43.4 0.0 reduce-scatter.3.cloned.1.call-update
  43.4 0.0 reduce-scatter.5.cloned.1.call-start
  43.5 0.0 copy-start.4
  43.5 0.6 copy-done.4
  44.1 0.6 dynamic-slice.2
  45.3 21.3 %all-reduce = f32[128]{0:T(128)S(1)} all-reduce(f32[128]{0:T(128)S(1)} %get-tuple-element.45), channel_id=3, replica_groups=mesh['dp'=8,'bank'=4] {'dp'}, use_global_device_ids=true, to_apply=%region_7.8.clone | all-reduce | flops 128 | bytes 1024
  66.7 0.1 dynamic-slice.3
  66.7 39.0 %reduce-scatter.3.cloned.1.call-done = f32[16,128]{1,0:T(8,128)} async-done(((f32[128,128]{1,0:T(8,128)}), f32[16,128]{1,0:T(8,128)}) %reduce-scatter.3.cloned.1.call-update) | async-done | bytes 8208 | tf_op jit(solution)/shard_map/reduce_scatter | solution.py:39
  105.7 6.0 %all-reduce.1 = (f32[16,128]{1,0:T(8,128)S(1)}, f32[16]{0:T(128)S(1)}) all-reduce(f32[16,128]{1,0:T(8,128)} %reduce-scatter.3.cloned.1.call-done, f32[16]{0:T(128)S(1)} %dynamic-slice.3), channel_id=1, replica_groups=mesh['dp'=8,'bank'=4] {'bank'}, use_global_device_ids=true, to_apply=%region_3.0 | all-reduce | flops 2064 | bytes 16512 | tf_op jit(solution)/shard_map/psum | solution.py:38
  111.7 0.2 multiply_reduce_fusion.5
  111.9 0.0 copy-start.2
  111.9 0.7 copy-done.2
  112.6 0.2 fusion.12
  112.8 0.0 copy-start.3
  112.8 0.2 convolution_bitcast_fusion.1
  113.0 0.5 copy-done.3
  113.5 0.7 add_add_fusion
  114.2 0.1 multiply_reduce_fusion.3
  114.3 0.2 multiply_reduce_fusion.8
  114.5 0.3 multiply_reduce_fusion.2
  114.8 30.5 %all_gather.7 = f32[128,128]{1,0:T(8,128)S(1)} all-gather(f32[16,128]{1,0:T(8,128)S(1)} %get-tuple-element.49), channel_id=1, replica_groups=mesh['dp'=8,'bank'=4] {'dp'}, dimensions={0}, use_global_device_ids=true | all-gather | bytes 73728 | tf_op jit(solution)/shard_map/all_gather | solution.py:69
  145.3 0.5 convolution_multiply_fusion
  145.8 1.1 fusion.24
  146.9 0.0 reduce-scatter.5.cloned.1.call-update
  147.0 60.8 %reduce-scatter.5.cloned.1.call-done = f32[16,128]{1,0:T(8,128)} async-done(((f32[128,128]{1,0:T(8,128)}), f32[16,128]{1,0:T(8,128)}) %reduce-scatter.5.cloned.1.call-update) | async-done | bytes 8208 | tf_op jit(solution)/shard_map/reduce_scatter | solution.py:39
  207.7 5.9 %psum.26 = f32[16,128]{1,0:T(8,128)S(1)} all-reduce(f32[16,128]{1,0:T(8,128)} %reduce-scatter.5.cloned.1.call-done), channel_id=1, replica_groups=mesh['dp'=8,'bank'=4] {'bank'}, use_global_device_ids=true, to_apply=%region_14.15 | all-reduce | flops 2048 | bytes 16384 | tf_op jit(solution)/shard_map/psum | solution.py:38
  213.6 0.3 multiply_reduce_fusion.1
  213.9 0.7 subtract_divide_fusion
  (6 shorter events, 0.0 us)
Async XLA Ops:
  7.2 34.5 %copy-start = (f32[512,128]{1,0:T(8,128)S(1)}, f32[512,128]{1,0:T(8,128)}, u32[]{:S(2)}) copy-start(f32[512,128]{1,0:T(8,128)} %param.6) | copy-start | bytes 786436
  7.2 98.6 %reduce-scatter.3.cloned.1.call-start = ((), (), s32[]{:S(2)}) async-start(), calls=%async_computation.2 | async-start | bytes 73728 | tf_op jit(solution)/shard_map/reduce_scatter | solution.py:39
  8.1 1.1 copy-start.1
  43.4 164.3 %reduce-scatter.5.cloned.1.call-start = ((), (), s32[]{:S(2)}) async-start(), calls=%async_computation.3 | async-start | bytes 73728 | tf_op jit(solution)/shard_map/reduce_scatter | solution.py:39
  43.5 0.7 copy-start.4
  111.9 0.7 copy-start.2
  112.8 0.7 copy-start.3
Sparse Core Ops, SparseCore 0:
  43.5 62.1 reduce-scatter.2
  147.1 60.5 reduce-scatter.4
where the time goes:
time: 222 us; the launch traced here: 221 us
  waiting for transfers between devices  99.8 us (45%)
  blocking collectives  95.9 us (43%)
  between operations  14.8 us (7%)
  matrix products  5.06 us (2%)
  other arithmetic  3.32 us (1%)
  local copies, waits for them, and re-layouts  2.43 us (1%)
    reduce_scatter x2, waiting for transfers between devices, reduce_owner(): return lax.psum_scatter(whole, 'dp', scatter_dimension=0, tiled=True)  99.7 us
    all_gather x1, blocking collectives, shards(): gathered = lax.all_gather(normed, 'dp', axis=0, tiled=True)  32.3 us
    all_gather x1, blocking collectives, shards(): gathered_grad = lax.all_gather(grad_soft, 'dp', axis=0, tiled=True)  30.5 us
    unnamed x1, blocking collectives  21.3 us
    psum x2, blocking collectives, reduce_owner(): whole = lax.psum(partials, 'bank')  11.8 us
  transfers between devices with their start and end apart: 2, of which 2 were waited for; matrix products, arithmetic and copies ran while one was open for 0% of the time, Pallas kernels for 0%

commit v1 on v0

--- a/solution.py
+++ b/solution.py
@@ -66,7 +66,12 @@
         normed,
     )
     grad_soft, grad_local = pullback(loss_weight)
-    gathered_grad = lax.all_gather(grad_soft, "dp", axis=0, tiled=True)
+    ring = [grad_soft]
+    for hop in range(7):
+        ring.append(lax.ppermute(ring[-1], "dp", [(dev, (dev + 1) % 8) for dev in range(8)]))
+    gathered_grad = jnp.roll(
+        jnp.concatenate(ring[::-1], axis=0), (lax.axis_index("dp") + 1) * ring[0].shape[0], axis=0
+    )
     grad_blocks = gathered_grad.reshape(-1, step_rows, width)
 
     def backward_block(paired):

time: 222 us -> 234 us (1.054)
  waiting for transfers between devices: 99.8 us -> 141 us
  blocking collectives: 95.9 us -> 65.4 us
    ppermute x0 -> x7, waiting for transfers between devices: none -> 43 us  [shards(): lax.ppermute(ring[-1], 'dp', [(dev, (dev + 1) % 8) for dev in range(8)])]
    all_gather x1 -> x0, blocking collectives: 30.5 us -> none  [shards(): gathered_grad = lax.all_gather(grad_soft, 'dp', axis=0, tiled=True)]
  transfers between devices with their start and end apart: 2 -> 9, of which waited for: 2 -> 9; matrix products, arithmetic and copies ran while one was open for 0% -> 0% of each run, Pallas kernels for 0% -> 0%
where the time goes in v1:
time: 234 us
  waiting for transfers between devices  141 us (60%)
  blocking collectives  65.4 us (28%)
  between operations  14.9 us (6%)
  matrix products  4.95 us (2%)
  other arithmetic  3.51 us (2%)
  local copies, waits for them, and re-layouts  2.47 us (1%)
    reduce_scatter x2, waiting for transfers between devices, reduce_owner(): return lax.psum_scatter(whole, 'dp', scatter_dimension=0, tiled=True)  98 us
    ppermute x7, waiting for transfers between devices, shards(): lax.ppermute(ring[-1], 'dp', [(dev, (dev + 1) % 8) for dev in range(8)])  43 us
    all_gather x1, blocking collectives, shards(): gathered = lax.all_gather(normed, 'dp', axis=0, tiled=True)  32.3 us
    unnamed x1, blocking collectives  21.3 us
    psum x2, blocking collectives, reduce_owner(): whole = lax.psum(partials, 'bank')  11.8 us
  transfers between devices with their start and end apart: 9, of which 9 were waited for; matrix products, arithmetic and copies ran while one was open for 0% of the time, Pallas kernels for 0%

profile of v1, /device:TPU:0, one launch (start us, length us, event | category | flops | bytes accessed | tf_op | source)
XLA Modules:
  0.0 233.8 jit_solution(18198492526490709803)
XLA Ops:
  7.2 0.0 copy-start
  7.2 0.0 reduce-scatter.3.cloned.1.call-start
  7.2 0.8 multiply_reduce_fusion.6
  8.1 1.1 multiply_reduce_fusion
  9.2 0.2 multiply_reduce_fusion.4
  9.4 32.3 %all_gather.3 = f32[128,128]{1,0:T(8,128)S(1)} all-gather(f32[16,128]{1,0:T(8,128)S(1)} %get-tuple-element.42), channel_id=1, replica_groups=mesh['dp'=8,'bank'=4] {'dp'}, dimensions={0}, use_global_device_ids=true | all-gather | bytes 73728 | tf_op jit(solution)/shard_map/all_gather | solution.py:49
  41.7 0.6 fusion.30
  42.3 1.1 fusion.27
  43.4 0.0 reduce-scatter.3.cloned.1.call-update
  43.4 0.0 reduce-scatter.5.cloned.1.call-start
  43.5 0.0 copy-start.4
  43.5 0.6 copy-done.4
  44.1 0.6 dynamic-slice.2
  45.4 21.3 %all-reduce = f32[128]{0:T(128)S(1)} all-reduce(f32[128]{0:T(128)S(1)} %get-tuple-element.47), channel_id=3, replica_groups=mesh['dp'=8,'bank'=4] {'dp'}, use_global_device_ids=true, to_apply=%region_7.8.clone | all-reduce | flops 128 | bytes 1024
  66.7 0.1 dynamic-slice.3
  66.7 39.0 %reduce-scatter.3.cloned.1.call-done = f32[16,128]{1,0:T(8,128)} async-done(((f32[128,128]{1,0:T(8,128)}), f32[16,128]{1,0:T(8,128)}) %reduce-scatter.3.cloned.1.call-update) | async-done | bytes 8208 | tf_op jit(solution)/shard_map/reduce_scatter | solution.py:39
  105.7 6.0 %all-reduce.1 = (f32[16,128]{1,0:T(8,128)S(1)}, f32[16]{0:T(128)S(1)}) all-reduce(f32[16,128]{1,0:T(8,128)} %reduce-scatter.3.cloned.1.call-done, f32[16]{0:T(128)S(1)} %dynamic-slice.3), channel_id=1, replica_groups=mesh['dp'=8,'bank'=4] {'bank'}, use_global_device_ids=true, to_apply=%region_3.0 | all-reduce | flops 2064 | bytes 16512 | tf_op jit(solution)/shard_map/psum | solution.py:38
  111.7 0.2 multiply_reduce_fusion.5
  111.9 0.7 copy-done.2
  112.6 0.2 fusion.13
  112.8 0.0 copy-start.3
  112.8 0.2 convolution_bitcast_fusion.1
  113.0 0.5 copy-done.3
  113.5 0.7 add_add_fusion
  114.2 0.1 multiply_reduce_fusion.3
  114.3 0.2 multiply_reduce_fusion.8
  114.5 0.2 convolution_add_fusion
  114.7 1.4 collective-permute-start
  116.1 4.9 %collective-permute-done = f32[16,128]{1,0:T(8,128)S(1)} collective-permute-done((f32[16,128]{1,0:T(8,128)S(1)}, f32[16,128]{1,0:T(8,128)S(1)}, u32[]{:S(2)}, u32[]{:S(2)}) %collective-permute-start) | collective-permute-done | bytes 8224 | tf_op jit(solution)/shard_map/ppermute | solution.py:71
  121.1 0.0 collective-permute-start.1
  121.1 6.3 %collective-permute-done.1 = f32[16,128]{1,0:T(8,128)S(1)} collective-permute-done((f32[16,128]{1,0:T(8,128)S(1)}, f32[16,128]{1,0:T(8,128)S(1)}, u32[]{:S(2)}, u32[]{:S(2)}) %collective-permute-start.1) | collective-permute-done | bytes 8224 | tf_op jit(solution)/shard_map/ppermute | solution.py:71
  127.4 0.0 collective-permute-start.2
  127.4 6.3 %collective-permute-done.2 = f32[16,128]{1,0:T(8,128)S(1)} collective-permute-done((f32[16,128]{1,0:T(8,128)S(1)}, f32[16,128]{1,0:T(8,128)S(1)}, u32[]{:S(2)}, u32[]{:S(2)}) %collective-permute-start.2) | collective-permute-done | bytes 8224 | tf_op jit(solution)/shard_map/ppermute | solution.py:71
  133.8 0.0 collective-permute-start.3
  133.8 6.3 %collective-permute-done.3 = f32[16,128]{1,0:T(8,128)S(1)} collective-permute-done((f32[16,128]{1,0:T(8,128)S(1)}, f32[16,128]{1,0:T(8,128)S(1)}, u32[]{:S(2)}, u32[]{:S(2)}) %collective-permute-start.3) | collective-permute-done | bytes 8224 | tf_op jit(solution)/shard_map/ppermute | solution.py:71
  140.1 0.0 collective-permute-start.4
  140.1 6.3 %collective-permute-done.4 = f32[16,128]{1,0:T(8,128)S(1)} collective-permute-done((f32[16,128]{1,0:T(8,128)S(1)}, f32[16,128]{1,0:T(8,128)S(1)}, u32[]{:S(2)}, u32[]{:S(2)}) %collective-permute-start.4) | collective-permute-done | bytes 8224 | tf_op jit(solution)/shard_map/ppermute | solution.py:71
  146.5 0.0 collective-permute-start.5
  146.5 6.3 %collective-permute-done.5 = f32[16,128]{1,0:T(8,128)S(1)} collective-permute-done((f32[16,128]{1,0:T(8,128)S(1)}, f32[16,128]{1,0:T(8,128)S(1)}, u32[]{:S(2)}, u32[]{:S(2)}) %collective-permute-start.5) | collective-permute-done | bytes 8224 | tf_op jit(solution)/shard_map/ppermute | solution.py:71
  152.8 6.3 %collective-permute-done.6 = f32[16,128]{1,0:T(8,128)S(1)} collective-permute-done((f32[16,128]{1,0:T(8,128)S(1)}, f32[16,128]{1,0:T(8,128)S(1)}, u32[]{:S(2)}, u32[]{:S(2)}) %collective-permute-start.6) | collective-permute-done | bytes 8224 | tf_op jit(solution)/shard_map/ppermute | solution.py:71
  159.2 0.2 multiply_reduce_fusion.2
  159.5 0.5 convolution_multiply_fusion
  160.0 1.1 fusion.26
  161.1 0.0 reduce-scatter.5.cloned.1.call-update
  161.1 59.0 %reduce-scatter.5.cloned.1.call-done = f32[16,128]{1,0:T(8,128)} async-done(((f32[128,128]{1,0:T(8,128)}), f32[16,128]{1,0:T(8,128)}) %reduce-scatter.5.cloned.1.call-update) | async-done | bytes 8208 | tf_op jit(solution)/shard_map/reduce_scatter | solution.py:39
  220.1 5.9 %psum.26 = f32[16,128]{1,0:T(8,128)S(1)} all-reduce(f32[16,128]{1,0:T(8,128)} %reduce-scatter.5.cloned.1.call-done), channel_id=1, replica_groups=mesh['dp'=8,'bank'=4] {'bank'}, use_global_device_ids=true, to_apply=%region_14.15 | all-reduce | flops 2048 | bytes 16384 | tf_op jit(solution)/shard_map/psum | solution.py:38
  225.9 0.3 multiply_reduce_fusion.1
  226.3 0.7 subtract_divide_fusion
  (26 shorter events, 0.1 us)
Async XLA Ops:
  7.2 34.5 %copy-start = (f32[512,128]{1,0:T(8,128)S(1)}, f32[512,128]{1,0:T(8,128)}, u32[]{:S(2)}) copy-start(f32[512,128]{1,0:T(8,128)} %param.6) | copy-start | bytes 786436
  7.2 98.6 %reduce-scatter.3.cloned.1.call-start = ((), (), s32[]{:S(2)}) async-start(), calls=%async_computation.2 | async-start | bytes 73728 | tf_op jit(solution)/shard_map/reduce_scatter | solution.py:39
  8.1 1.1 copy-start.1
  43.4 176.7 %reduce-scatter.5.cloned.1.call-start = ((), (), s32[]{:S(2)}) async-start(), calls=%async_computation.3 | async-start | bytes 73728 | tf_op jit(solution)/shard_map/reduce_scatter | solution.py:39
  43.5 0.7 copy-start.4
  111.9 0.7 copy-start.2
  112.8 0.7 copy-start.3
  114.7 6.4 %collective-permute-start = (f32[16,128]{1,0:T(8,128)S(1)}, f32[16,128]{1,0:T(8,128)S(1)}, u32[]{:S(2)}, u32[]{:S(2)}) collective-permute-start(f32[16,128]{1,0:T(8,128)S(1)} %convolution_add_fusion), channel_id=1, source_target_pairs={{0,4},{4,8},{8,12},{12,16},{16,20},{20,24},{24,28},{28,0},{1,5},{5... | collective-permute-start | bytes 24584 | tf_op jit(solution)/shard_map/ppermute | solution.py:71
  121.1 6.3 %collective-permute-start.1 = (f32[16,128]{1,0:T(8,128)S(1)}, f32[16,128]{1,0:T(8,128)S(1)}, u32[]{:S(2)}, u32[]{:S(2)}) collective-permute-start(f32[16,128]{1,0:T(8,128)S(1)} %collective-permute-done), channel_id=1, source_target_pairs={{0,4},{4,8},{8,12},{12,16},{16,20},{20,24},{24,28},{28,0},{1,5},{5... | collective-permute-start | bytes 24584 | tf_op jit(solution)/shard_map/ppermute | solution.py:71
  127.4 6.3 %collective-permute-start.2 = (f32[16,128]{1,0:T(8,128)S(1)}, f32[16,128]{1,0:T(8,128)S(1)}, u32[]{:S(2)}, u32[]{:S(2)}) collective-permute-start(f32[16,128]{1,0:T(8,128)S(1)} %collective-permute-done.1), channel_id=1, source_target_pairs={{0,4},{4,8},{8,12},{12,16},{16,20},{20,24},{24,28},{28,0},{1,5},{5... | collective-permute-start | bytes 24584 | tf_op jit(solution)/shard_map/ppermute | solution.py:71
  133.8 6.3 %collective-permute-start.3 = (f32[16,128]{1,0:T(8,128)S(1)}, f32[16,128]{1,0:T(8,128)S(1)}, u32[]{:S(2)}, u32[]{:S(2)}) collective-permute-start(f32[16,128]{1,0:T(8,128)S(1)} %collective-permute-done.2), channel_id=1, source_target_pairs={{0,4},{4,8},{8,12},{12,16},{16,20},{20,24},{24,28},{28,0},{1,5},{5... | collective-permute-start | bytes 24584 | tf_op jit(solution)/shard_map/ppermute | solution.py:71
  140.1 6.3 %collective-permute-start.4 = (f32[16,128]{1,0:T(8,128)S(1)}, f32[16,128]{1,0:T(8,128)S(1)}, u32[]{:S(2)}, u32[]{:S(2)}) collective-permute-start(f32[16,128]{1,0:T(8,128)S(1)} %collective-permute-done.3), channel_id=1, source_target_pairs={{0,4},{4,8},{8,12},{12,16},{16,20},{20,24},{24,28},{28,0},{1,5},{5... | collective-permute-start | bytes 24584 | tf_op jit(solution)/shard_map/ppermute | solution.py:71
  146.5 6.3 %collective-permute-start.5 = (f32[16,128]{1,0:T(8,128)S(1)}, f32[16,128]{1,0:T(8,128)S(1)}, u32[]{:S(2)}, u32[]{:S(2)}) collective-permute-start(f32[16,128]{1,0:T(8,128)S(1)} %collective-permute-done.4), channel_id=1, source_target_pairs={{0,4},{4,8},{8,12},{12,16},{16,20},{20,24},{24,28},{28,0},{1,5},{5... | collective-permute-start | bytes 24584 | tf_op jit(solution)/shard_map/ppermute | solution.py:71
  152.8 6.3 %collective-permute-start.6 = (f32[16,128]{1,0:T(8,128)S(1)}, f32[16,128]{1,0:T(8,128)S(1)}, u32[]{:S(2)}, u32[]{:S(2)}) collective-permute-start(f32[16,128]{1,0:T(8,128)S(1)} %collective-permute-done.5), channel_id=1, source_target_pairs={{0,4},{4,8},{8,12},{12,16},{16,20},{20,24},{24,28},{28,0},{1,5},{5... | collective-permute-start | bytes 24584 | tf_op jit(solution)/shard_map/ppermute | solution.py:71
Sparse Core Ops, SparseCore 0:
  43.5 62.1 reduce-scatter.2
  161.2 58.8 reduce-scatter.4
